TPU v7x, 512 devices: a whole 4x8x8 slice. The times are simulated.
512 devices in a mesh: grp: 16 (over z, core), seq: 32 (over y, x).
Axes of the slice: x: 4, y: 8, z: 8, core: 2. Of those that a mesh axis runs over, the one named last changes fastest.
Arguments:
- queries: bfloat16 [32, 32, 64, 1536], P('grp', 'seq'), may hold values from -100 to 100
- keys: bfloat16 [32, 32, 64, 1536], P('grp', 'seq'), may hold values from -5 to 5
- values: bfloat16 [32, 32, 64, 1536], P('grp', 'seq'), may hold values from -6 to 6
- grad_out: bfloat16 [32, 32, 64, 1536], P('grp', 'seq'), may hold values from -6 to 6
- frames: int32 [32], replicated, may hold values from 1 to 32
- timesteps: int32 [32], replicated, may hold values from 0 to 999
- order: int32 [16, 2], replicated, may hold values from 0 to 1, each once within a row
- gate_weight: bfloat16 [256, 1536], replicated, may hold values from -0.375 to 0.375
Outputs:
- attn_out: bfloat16 [32, 32, 64, 1536], P('grp', 'seq')
- grad_q: bfloat16 [32, 32, 64, 1536], P('grp', 'seq')
- grad_k: bfloat16 [32, 32, 64, 1536], P('grp', 'seq')
- grad_v: bfloat16 [32, 32, 64, 1536], P('grp', 'seq')
- grad_gate: bfloat16 [256, 1536], replicated
All inputs are finite; a program needn't handle non-finite values.
Results may differ from a plain program's by a relative error of at most 0.012.
Values may be sent and summed in bfloat16 or wider, within the bound.
A program may use at most 64 MiB of HBM per device.

v0:
```python
import functools
import math

import jax
import jax.numpy as jnp
from jax import lax
from jax.experimental import pallas as pl
from jax.experimental.pallas import tpu as pltpu
from jax.sharding import PartitionSpec as P

MESH = pl.DeviceIdType.MESH
HD = 128
ROWS = 16
CUT = 3
GROUPS, RANKS = 16, 32
SPAN = CUT * HD
PACK = 4
SIDE = PACK * RANKS
NT = (((1,), (1,)), ((), ()))
TN = (((0,), (0,)), ((), ()))
NN = (((1,), (0,)), ((), ()))


def dot(a, b, dims):
    return lax.dot_general(a, b, dims, preferred_element_type=jnp.float32)


def exchange(
    frames, steps, order, q_ref, k_ref, v_ref, go_ref, gw_ref,
    outs_ref, sums_ref, emb_ref,
    raw, stage, rin, ob, xf, of, gwv, gate, part, seen, own, everyone,
    load_sem, ssem, rsem, osend, orecv, asend, arecv, bsend, brecv,
):
    g = lax.axis_index("grp")
    me = lax.axis_index("seq")
    partner = lax.rem(g + GROUPS // 2, GROUPS)
    clip = me // 16
    block = lax.rem(me // 4, 4)
    heads = lax.rem(me, 4)

    barrier = pltpu.get_barrier_semaphore()

    def greet(grp, seq):
        pl.semaphore_signal(barrier, inc=1, device_id=(grp, seq), device_id_type=MESH)

    @pl.loop(1, RANKS)
    def _(o):
        greet(g, lax.rem(me + o, RANKS))

    @pl.when(clip == 1)
    def _():
        @pl.loop(0, RANKS)
        def _(o):
            greet(partner, lax.rem(me + o, RANKS))

    @pl.loop(1, GROUPS)
    def _(o):
        greet(lax.rem(g + o, GROUPS), me)

    loads = [
        pltpu.make_async_copy(ref, raw.at[t], load_sem.at[t])
        for t, ref in enumerate((q_ref, k_ref, v_ref))
    ]
    for r in range(2):
        loads.append(pltpu.make_async_copy(go_ref.at[r], stage.at[r, 3], load_sem.at[3 + r]))
    mine = pl.ds(pl.multiple_of(heads * SPAN, HD), SPAN)
    weight = pltpu.make_async_copy(gw_ref.at[:, mine], gwv, load_sem.at[5])
    for load in loads:
        load.start()
    weight.start()
    for load in loads:
        load.wait()
    for t in range(3):
        for r in range(2):
            stage[r, t] = raw[t, order[g, r]]
    pl.semaphore_wait(barrier, RANKS - 1 + 16 + GROUPS - 1)

    def out_to(h, j, t0, n):
        r, b, w = j // 16, lax.rem(j // 4, 4), lax.rem(j, 4)
        return stage.at[
            r,
            pl.ds(t0, n),
            pl.ds(pl.multiple_of(b * ROWS, ROWS), ROWS),
            pl.ds(pl.multiple_of(w * SPAN + h * HD, HD), HD),
        ]

    def slot(h, f, t0, n):
        return rin.at[pl.ds(h * (RANKS * 4) + f * 4 + t0, n)]

    def send(h, j, grp, t0, n):
        pltpu.make_async_remote_copy(
            src_ref=out_to(h, j, t0, n),
            dst_ref=slot(h, me, t0, n),
            send_sem=ssem,
            recv_sem=rsem.at[h],
            device_id=(grp, j),
            device_id_type=MESH,
        ).start()

    def keep(h, t0, n):
        pltpu.make_async_copy(out_to(h, me, t0, n), slot(h, me, t0, n), rsem.at[h]).start()

    @pl.loop(0, CUT)
    def _(h):
        @pl.loop(1, RANKS)
        def _(o):
            j = lax.rem(me + o, RANKS)

            @pl.when(j < 16)
            def _():
                send(h, j, g, 0, 4)

            @pl.when(j >= 16)
            def _():
                send(h, j, partner, 0, 3)
                send(h, j, g, 3, 1)

        @pl.when(clip == 0)
        def _():
            keep(h, 0, 4)

        @pl.when(clip == 1)
        def _():
            send(h, me, partner, 0, 3)
            keep(h, 3, 1)

    half = HD
    row = lax.broadcasted_iota(jnp.int32, (2 * GROUPS, half), 0)
    stamp = jnp.zeros((2 * GROUPS, half), jnp.float32)
    for c in range(2 * GROUPS):
        src = c // 2 if c % 2 == 0 else (c // 2 + GROUPS // 2) % GROUPS
        anchor = src * 2 + order[src, c % 2]
        stamp = jnp.where(row == c, steps[anchor].astype(jnp.float32), stamp)
    k = lax.broadcasted_iota(jnp.int32, (2 * GROUPS, half), 1).astype(jnp.float32)
    angle = stamp * jnp.exp(-math.log(10000.0) * k / half)
    emb_ref[:, :half] = jnp.cos(angle)
    emb_ref[:, half:] = jnp.sin(angle)
    weight.wait()
    gates = lax.dot_general(
        emb_ref[...],
        gwv[...].astype(jnp.float32),
        NN,
        precision=lax.Precision.HIGHEST,
        preferred_element_type=jnp.float32,
    )
    pick = lax.broadcasted_iota(jnp.int32, gates.shape, 0) == g * 2 + clip
    gate[...] = jnp.broadcast_to(
        jnp.sum(jnp.where(pick, gates, 0.0), axis=0, keepdims=True), gate.shape
    )
    source = jnp.where(clip == 0, g, partner)
    count = frames[source * 2 + order[source, clip]]

    line = lax.broadcasted_iota(jnp.int32, (SIDE, SIDE), 0)
    lane = lax.broadcasted_iota(jnp.int32, (SIDE, SIDE), 1)
    live = (line // RANKS == lane // RANKS) & (lax.rem(lane, RANKS) < count)
    asks = (
        lax.rem(lax.broadcasted_iota(jnp.int32, (SIDE, HD), 0), RANKS) < count
    ).astype(jnp.float32)
    scale = HD ** (-0.5)

    @pl.loop(0, CUT)
    def _(h):
        base = h * (RANKS * 4)
        pltpu.make_async_copy(
            rin.at[pl.ds(base, RANKS * 4)], rin.at[pl.ds(base, RANKS * 4)], rsem.at[h]
        ).wait()
        for f in range(RANKS):
            for t in range(4):
                xf[t, f * ROWS : (f + 1) * ROWS, :] = rin[base + f * 4 + t].astype(jnp.float32)
        lanes = pl.ds(pl.multiple_of(h * HD, HD), HD)
        gate_h = gate[0:1, lanes]
        total = jnp.zeros((1, HD), jnp.float32)
        for s in range(ROWS // PACK):

            def take(t):
                return jnp.concatenate(
                    [xf[t, pl.ds(s * PACK + p, RANKS, stride=ROWS), :] for p in range(PACK)], axis=0
                )

            def put(t, value):
                for p in range(PACK):
                    of[t, pl.ds(s * PACK + p, RANKS, stride=ROWS), :] = value[
                        p * RANKS : (p + 1) * RANKS
                    ]

            query = take(0).astype(jnp.bfloat16)
            key = take(1).astype(jnp.bfloat16)
            value = take(2).astype(jnp.bfloat16)
            cotan = take(3)
            scores = jnp.where(live, dot(query, key, NT) * scale, -jnp.inf)
            top = jnp.max(scores, axis=-1, keepdims=True)
            expo = jnp.where(live, jnp.exp(scores - top), 0.0)
            probs = expo / jnp.sum(expo, axis=-1, keepdims=True)
            probs_b = probs.astype(jnp.bfloat16)
            attn = dot(probs_b, value, NN) * asks
            put(0, gate_h * attn)
            total = total + jnp.sum(cotan * attn, axis=0, keepdims=True)
            grad_a = (cotan * gate_h * asks).astype(jnp.bfloat16)
            put(3, dot(probs_b, grad_a, TN))
            dprobs = dot(grad_a, value, NT)
            diag = jnp.sum(probs * dprobs, axis=-1, keepdims=True)
            dscores = (probs * (dprobs - diag)).astype(jnp.bfloat16)
            put(1, dot(dscores, key, NN) * scale)
            put(2, dot(dscores, query, TN) * scale)
        part[0:1, lanes] = total
        for f in range(RANKS):
            for t in range(4):
                ob[base + f * 4 + t] = of[t, f * ROWS : (f + 1) * ROWS, :].astype(jnp.bfloat16)

        @pl.when(h == CUT - 1)
        def _():
            seen[me] = part[...]

            @pl.loop(1, RANKS)
            def _(o):
                pltpu.make_async_remote_copy(
                    src_ref=part,
                    dst_ref=seen.at[me],
                    send_sem=asend,
                    recv_sem=arecv,
                    device_id=(g, lax.rem(me + o, RANKS)),
                    device_id_type=MESH,
                ).start()

        place = outs_ref.at[
            :,
            clip,
            pl.ds(pl.multiple_of(block * ROWS, ROWS), ROWS),
            pl.ds(pl.multiple_of(heads * SPAN + h * HD, HD), HD),
        ]

        @pl.loop(1, RANKS)
        def _(o):
            f = lax.rem(me + o, RANKS)
            pltpu.make_async_remote_copy(
                src_ref=ob.at[pl.ds(base + f * 4, 4)],
                dst_ref=place,
                send_sem=osend,
                recv_sem=orecv,
                device_id=(g, f),
                device_id_type=MESH,
            ).start()

        pltpu.make_async_copy(ob.at[pl.ds(base + me * 4, 4)], place, orecv).start()

    few = seen.at[pl.ds(0, RANKS - 1)]
    pltpu.make_async_copy(few, few, arecv).wait()
    for r in range(2):
        for w in range(4):
            acc = seen[r * 16 + w]
            for b in range(1, 4):
                acc = acc + seen[r * 16 + b * 4 + w]
            own[w * 2 + r : w * 2 + r + 1, :] = acc
    everyone[g] = own[...]

    @pl.loop(1, GROUPS)
    def _(o):
        pltpu.make_async_remote_copy(
            src_ref=own,
            dst_ref=everyone.at[g],
            send_sem=bsend,
            recv_sem=brecv,
            device_id=(lax.rem(g + o, GROUPS), me),
            device_id_type=MESH,
        ).start()

    others = everyone.at[pl.ds(0, GROUPS - 1)]
    pltpu.make_async_copy(others, others, brecv).wait()
    for i in range(GROUPS):
        for w in range(4):
            sums_ref[w, 2 * i : 2 * i + 2, :] = everyone[i, 2 * w : 2 * w + 2, :]

    def drain(sem, ref):
        pltpu.make_async_copy(ref, ref, sem).wait()

    drain(asend, few)
    drain(bsend, others)

    @pl.when(clip == 0)
    def _():
        drain(ssem, rin.at[pl.ds(0, CUT * (15 * 4 + 16 * 4))])

    @pl.when(clip == 1)
    def _():
        drain(ssem, rin.at[pl.ds(0, CUT * (16 * 4 + 15 + 16 * 3))])

    drain(osend, rin.at[pl.ds(0, CUT * (RANKS - 1) * 4)])
    drain(orecv, outs_ref)


def finish(outs_ref, sums_ref, emb_ref, o_ref, q_ref, k_ref, v_ref, gg_ref, sem):
    copies = [
        pltpu.make_async_copy(outs_ref.at[t], ref, sem.at[t])
        for t, ref in enumerate((o_ref, q_ref, k_ref, v_ref))
    ]
    for copy in copies:
        copy.start()
    emb = emb_ref[...]
    for w in range(4):
        clips = sums_ref[w]
        gg_ref[:, w * SPAN : (w + 1) * SPAN] = lax.dot_general(
            emb,
            clips,
            TN,
            precision=lax.Precision.HIGHEST,
            preferred_element_type=jnp.float32,
        ).astype(jnp.bfloat16)
    for copy in copies:
        copy.wait()


def body(queries, keys, values, grad_out, frames, timesteps, order, gate_weight):
    clips, fr_dev, spots, width = queries.shape
    flat = (clips, spots, width)
    any_space = pl.BlockSpec(memory_space=pl.ANY)
    smem = pl.BlockSpec(memory_space=pltpu.SMEM)
    vmem = pl.BlockSpec(memory_space=pltpu.VMEM)
    bf16, f32 = jnp.bfloat16, jnp.float32
    dma = pltpu.SemaphoreType.DMA
    outs, sums, emb = pl.pallas_call(
        exchange,
        out_shape=(
            jax.ShapeDtypeStruct((4,) + flat, bf16),
            jax.ShapeDtypeStruct((4, 2 * GROUPS, SPAN), f32),
            jax.ShapeDtypeStruct((2 * GROUPS, 2 * HD), f32),
        ),
        in_specs=[smem] * 3 + [any_space] * 5,
        out_specs=(any_space, vmem, vmem),
        scratch_shapes=[
            pltpu.VMEM((3,) + flat, bf16),
            pltpu.VMEM((2, 4, spots, width), bf16),
            pltpu.VMEM((CUT * RANKS * 4, ROWS, HD), bf16),
            pltpu.VMEM((CUT * RANKS * 4, ROWS, HD), bf16),
            pltpu.VMEM((4, RANKS * ROWS, HD), f32),
            pltpu.VMEM((4, RANKS * ROWS, HD), f32),
            pltpu.VMEM((gate_weight.shape[0], SPAN), bf16),
            pltpu.VMEM((8, SPAN), f32),
            pltpu.VMEM((1, SPAN), f32),
            pltpu.VMEM((RANKS, 1, SPAN), f32),
            pltpu.VMEM((8, SPAN), f32),
            pltpu.VMEM((GROUPS, 8, SPAN), f32),
            dma((6,)),
            dma,
            dma((CUT,)),
            dma,
            dma,
            dma,
            dma,
            dma,
            dma,
        ],
        compiler_params=pltpu.CompilerParams(
            collective_id=0, has_side_effects=True, vmem_limit_bytes=32 << 20
        ),
    )(
        frames,
        timesteps,
        order,
        queries.reshape(flat),
        keys.reshape(flat),
        values.reshape(flat),
        grad_out.reshape(flat),
        gate_weight,
    )
    results = pl.pallas_call(
        finish,
        out_shape=tuple(jax.ShapeDtypeStruct(flat, bf16) for _ in range(4))
        + (jax.ShapeDtypeStruct(gate_weight.shape, bf16),),
        in_specs=[any_space, vmem, vmem],
        out_specs=(any_space,) * 4 + (vmem,),
        scratch_shapes=[dma((4,))],
        compiler_params=pltpu.CompilerParams(vmem_limit_bytes=32 << 20),
    )(outs, sums, emb)
    back = tuple(x.reshape(clips, fr_dev, spots, width) for x in results[:4])
    return back + (results[4],)


def solution(mesh):
    split = P("grp", "seq", None, None)
    return jax.shard_map(
        body,
        mesh=mesh,
        in_specs=(split,) * 4 + (P(),) * 4,
        out_specs=(split,) * 4 + (P(),),
        check_vma=False,
    )
```

profile of v0, /device:TPU:1, one launch (start us, length us, event | category | flops | bytes accessed | tf_op | source)
XLA Modules:
  0.0 122.7 jit_solution(4211315971046448785)
XLA Ops:
  0.6 0.8 copy.13.order
  1.4 0.0 copy-start
  1.4 1.1 copy-done
  2.5 0.0 copy-start.1
  2.5 1.0 copy-done.1
  3.5 0.0 copy-start.2
  3.5 1.0 copy-done.2
  4.5 0.0 copy-start.3
  4.5 1.0 copy-done.3
  5.5 0.0 copy-start.4
  5.5 1.0 copy-done.4
  6.5 0.0 copy-start.5
  6.5 0.7 copy-done.5
  7.2 0.0 copy-start.6
  7.2 0.7 copy-done.6
  7.8 112.5 %shard_map.119 = (bf16[4,2,64,1536]{3,2,1,0:T(8,128)(2,1)S(1)}, f32[4,32,384]{2,1,0:T(8,128)S(1)}, f32[32,256]{1,0:T(8,128)S(1)}) custom-call(s32[32]{0:T(128)S(1)} %copy-done.5, s32[32]{0:T(128)S(1)} %copy-done.6, s32[16,2]{1,0:T(8,128)S(1)} %copy.13.order, bf16[2,64,1536]{2,1,0:T(8,128)(2,1)S(1)} %bitcast.16, bf16[2,64,1536]{2,1,0:T(8,128)(2,1)S(1)} %bitcast.17, ...), custom_call_target="tpu_custom_call" | custom-call | tf_op jit(solution)/shard_map/pallas_call | solution.py:320
  120.4 2.4 %shard_map.120 = (bf16[2,64,1536]{2,1,0:T(8,128)(2,1)}, bf16[2,64,1536]{2,1,0:T(8,128)(2,1)}, bf16[2,64,1536]{2,1,0:T(8,128)(2,1)}, bf16[2,64,1536]{2,1,0:T(8,128)(2,1)}, bf16[256,1536]{1,0:T(8,128)(2,1)}) custom-call(bf16[4,2,64,1536]{3,2,1,0:T(8,128)(2,1)S(1)} %get-tuple-element.13.outs_ref, f32[4,32,384]{2,1,0:T(8,128)S(1)} %get-tuple-element.14.sums_ref, ...), custom_call_target="tpu_custom_call" | custom-call | tf_op jit(solution)/shard_map/pallas_call | solution.py:365
Async XLA Ops:
  1.4 1.1 copy-start
  2.5 1.0 copy-start.1
  3.5 1.0 copy-start.2
  4.5 1.0 copy-start.3
  5.5 1.0 copy-start.4
  6.5 0.7 copy-start.5
  7.2 0.7 copy-start.6
where the time goes:
time: 123 us
  Pallas kernels  115 us (93%)
  local copies, waits for them, and re-layouts  7.18 us (6%)
    pallas_call x1, Pallas kernels, body(): pl.pallas_call(exchange, out_shape=(jax.ShapeDtypeStruct((4,) + flat, bf1...  113 us
    unnamed x15, local copies, waits for them, and re-layouts  7.18 us

commit v1 on v0

--- a/solution.py
+++ b/solution.py
@@ -10,6 +10,8 @@
 
 MESH = pl.DeviceIdType.MESH
 HD = 128
+ZSPLIT = False
+EARLY = False
 ROWS = 16
 CUT = 3
 GROUPS, RANKS = 16, 32
@@ -28,8 +30,8 @@
 def exchange(
     frames, steps, order, q_ref, k_ref, v_ref, go_ref, gw_ref,
     outs_ref, sums_ref, emb_ref,
-    raw, stage, rin, ob, xf, of, gwv, gate, part, seen, own, everyone,
-    load_sem, ssem, rsem, osend, orecv, asend, arecv, bsend, brecv,
+    raw, stage, moved, rin, ob, xf, of, gwv, gate, part, seen, own, everyone,
+    load_sem, zsend, zrecv, ssem, rsem, osend, orecv, asend, arecv, bsend, brecv,
 ):
     g = lax.axis_index("grp")
     me = lax.axis_index("seq")
@@ -38,6 +40,16 @@
     block = lax.rem(me // 4, 4)
     heads = lax.rem(me, 4)
 
+    loads = [
+        pltpu.make_async_copy(ref, raw.at[t], load_sem.at[t])
+        for t, ref in enumerate((q_ref, k_ref, v_ref, go_ref))
+    ]
+    mine = pl.ds(pl.multiple_of(heads * SPAN, HD), SPAN)
+    weight = pltpu.make_async_copy(gw_ref.at[:, mine], gwv, load_sem.at[4])
+    for load in loads:
+        load.start()
+    weight.start()
+
     barrier = pltpu.get_barrier_semaphore()
 
     def greet(grp, seq):
@@ -47,89 +59,117 @@
     def _(o):
         greet(g, lax.rem(me + o, RANKS))
 
-    @pl.when(clip == 1)
-    def _():
-        @pl.loop(0, RANKS)
-        def _(o):
-            greet(partner, lax.rem(me + o, RANKS))
-
     @pl.loop(1, GROUPS)
     def _(o):
         greet(lax.rem(g + o, GROUPS), me)
 
-    loads = [
-        pltpu.make_async_copy(ref, raw.at[t], load_sem.at[t])
-        for t, ref in enumerate((q_ref, k_ref, v_ref))
-    ]
-    for r in range(2):
-        loads.append(pltpu.make_async_copy(go_ref.at[r], stage.at[r, 3], load_sem.at[3 + r]))
-    mine = pl.ds(pl.multiple_of(heads * SPAN, HD), SPAN)
-    weight = pltpu.make_async_copy(gw_ref.at[:, mine], gwv, load_sem.at[5])
-    for load in loads:
-        load.start()
-    weight.start()
     for load in loads:
         load.wait()
-    for t in range(3):
-        for r in range(2):
-            stage[r, t] = raw[t, order[g, r]]
-    pl.semaphore_wait(barrier, RANKS - 1 + 16 + GROUPS - 1)
-
-    def out_to(h, j, t0, n):
-        r, b, w = j // 16, lax.rem(j // 4, 4), lax.rem(j, 4)
-        return stage.at[
-            r,
-            pl.ds(t0, n),
-            pl.ds(pl.multiple_of(b * ROWS, ROWS), ROWS),
-            pl.ds(pl.multiple_of(w * SPAN + h * HD, HD), HD),
-        ]
+
+    def rows(b):
+        return pl.ds(pl.multiple_of(b * ROWS, ROWS), ROWS)
 
     def slot(h, f, t0, n):
         return rin.at[pl.ds(h * (RANKS * 4) + f * 4 + t0, n)]
 
-    def send(h, j, grp, t0, n):
+    def send(h, j, t0, src):
         pltpu.make_async_remote_copy(
-            src_ref=out_to(h, j, t0, n),
-            dst_ref=slot(h, me, t0, n),
+            src_ref=src,
+            dst_ref=slot(h, me, t0, src.shape[0]),
             send_sem=ssem,
             recv_sem=rsem.at[h],
-            device_id=(grp, j),
+            device_id=(g, j),
             device_id_type=MESH,
         ).start()
 
-    def keep(h, t0, n):
-        pltpu.make_async_copy(out_to(h, me, t0, n), slot(h, me, t0, n), rsem.at[h]).start()
-
-    @pl.loop(0, CUT)
-    def _(h):
-        @pl.loop(1, RANKS)
+    def keep(h, t0, src):
+        pltpu.make_async_copy(src, slot(h, me, t0, src.shape[0]), rsem.at[h]).start()
+
+    def migrate(h, src, dst):
+        pltpu.make_async_remote_copy(
+            src_ref=src,
+            dst_ref=dst,
+            send_sem=zsend,
+            recv_sem=zrecv.at[h],
+            device_id=(partner, me),
+            device_id_type=MESH,
+        ).start()
+
+    def arrange(h):
+        for r in range(2):
+            for t in range(4):
+                which = order[r, g] if t < 3 else r
+                for w in range(4):
+                    lanes = slice(w * SPAN + h * HD, w * SPAN + h * HD + HD)
+                    stage[h, r, t, w] = raw[t, which, :, lanes]
+
+    def plane(h):
+        if not ZSPLIT:
+            migrate(h, stage.at[h, 1, pl.ds(0, 3)], moved.at[h])
+
+        @pl.loop(0, RANKS)
         def _(o):
             j = lax.rem(me + o, RANKS)
-
-            @pl.when(j < 16)
-            def _():
-                send(h, j, g, 0, 4)
-
-            @pl.when(j >= 16)
-            def _():
-                send(h, j, partner, 0, 3)
-                send(h, j, g, 3, 1)
-
-        @pl.when(clip == 0)
-        def _():
-            keep(h, 0, 4)
-
-        @pl.when(clip == 1)
-        def _():
-            send(h, me, partner, 0, 3)
-            keep(h, 3, 1)
+            b, w = lax.rem(j // 4, 4), lax.rem(j, 4)
+            if ZSPLIT:
+                @pl.when(lax.rem(o, 2) == 0)
+                def _():
+                    pb, pw = o // 8, lax.rem(o // 2, 4)
+                    migrate(
+                        h,
+                        stage.at[h, 1, pl.ds(0, 3), pw, rows(pb)],
+                        moved.at[h, :, pw, rows(pb)],
+                    )
+
+            @pl.when((j < 16) & (o > 0))
+            def _():
+                send(h, j, 0, stage.at[h, 0, pl.ds(0, 4), w, rows(b)])
+
+            @pl.when((j >= 16) & (o > 0))
+            def _():
+                send(h, j, 3, stage.at[h, 1, pl.ds(3, 1), w, rows(b)])
+
+            @pl.when((j < 16) & (o == 0))
+            def _():
+                keep(h, 0, stage.at[h, 0, pl.ds(0, 4), w, rows(b)])
+
+            @pl.when((j >= 16) & (o == 0))
+            def _():
+                keep(h, 3, stage.at[h, 1, pl.ds(3, 1), w, rows(b)])
+
+    def forward(h):
+        pltpu.make_async_copy(moved.at[h], moved.at[h], zrecv.at[h]).wait()
+
+        @pl.loop(0, 16)
+        def _(o):
+            i = lax.rem(me + o, 16)
+            j = 16 + i
+            b, w = i // 4, lax.rem(i, 4)
+
+            @pl.when(j != me)
+            def _():
+                send(h, j, 0, moved.at[h, :, w, rows(b)])
+
+            @pl.when(j == me)
+            def _():
+                keep(h, 0, moved.at[h, :, w, rows(b)])
+
+    arrange(0)
+    pl.semaphore_wait(barrier, RANKS - 1 + GROUPS - 1)
+    plane(0)
+    arrange(1)
+    plane(1)
+    arrange(2)
+    if EARLY:
+        forward(0)
+    plane(2)
 
     half = HD
     row = lax.broadcasted_iota(jnp.int32, (2 * GROUPS, half), 0)
     stamp = jnp.zeros((2 * GROUPS, half), jnp.float32)
     for c in range(2 * GROUPS):
         src = c // 2 if c % 2 == 0 else (c // 2 + GROUPS // 2) % GROUPS
-        anchor = src * 2 + order[src, c % 2]
+        anchor = src * 2 + order[c % 2, src]
         stamp = jnp.where(row == c, steps[anchor].astype(jnp.float32), stamp)
     k = lax.broadcasted_iota(jnp.int32, (2 * GROUPS, half), 1).astype(jnp.float32)
     angle = stamp * jnp.exp(-math.log(10000.0) * k / half)
@@ -148,7 +188,12 @@
         jnp.sum(jnp.where(pick, gates, 0.0), axis=0, keepdims=True), gate.shape
     )
     source = jnp.where(clip == 0, g, partner)
-    count = frames[source * 2 + order[source, clip]]
+    count = frames[source * 2 + order[clip, source]]
+
+    if not EARLY:
+        forward(0)
+    forward(1)
+    forward(2)
 
     line = lax.broadcasted_iota(jnp.int32, (SIDE, SIDE), 0)
     lane = lax.broadcasted_iota(jnp.int32, (SIDE, SIDE), 1)
@@ -276,14 +321,8 @@
     drain(asend, few)
     drain(bsend, others)
 
-    @pl.when(clip == 0)
-    def _():
-        drain(ssem, rin.at[pl.ds(0, CUT * (15 * 4 + 16 * 4))])
-
-    @pl.when(clip == 1)
-    def _():
-        drain(ssem, rin.at[pl.ds(0, CUT * (16 * 4 + 15 + 16 * 3))])
-
+    drain(zsend, moved)
+    drain(ssem, rin.at[pl.ds(0, CUT * (RANKS - 1) * 4)])
     drain(osend, rin.at[pl.ds(0, CUT * (RANKS - 1) * 4)])
     drain(orecv, outs_ref)
 
@@ -327,8 +366,9 @@
         in_specs=[smem] * 3 + [any_space] * 5,
         out_specs=(any_space, vmem, vmem),
         scratch_shapes=[
-            pltpu.VMEM((3,) + flat, bf16),
-            pltpu.VMEM((2, 4, spots, width), bf16),
+            pltpu.VMEM((4,) + flat, bf16),
+            pltpu.VMEM((CUT, 2, 4, 4, spots, HD), bf16),
+            pltpu.VMEM((CUT, 3, 4, spots, HD), bf16),
             pltpu.VMEM((CUT * RANKS * 4, ROWS, HD), bf16),
             pltpu.VMEM((CUT * RANKS * 4, ROWS, HD), bf16),
             pltpu.VMEM((4, RANKS * ROWS, HD), f32),
@@ -339,7 +379,9 @@
             pltpu.VMEM((RANKS, 1, SPAN), f32),
             pltpu.VMEM((8, SPAN), f32),
             pltpu.VMEM((GROUPS, 8, SPAN), f32),
-            dma((6,)),
+            dma((5,)),
+            dma,
+            dma((CUT,)),
             dma,
             dma((CUT,)),
             dma,
@@ -355,12 +397,12 @@
     )(
         frames,
         timesteps,
-        order,
-        queries.reshape(flat),
-        keys.reshape(flat),
-        values.reshape(flat),
-        grad_out.reshape(flat),
-        gate_weight,
+        order.T,
+        pltpu.with_memory_space_constraint(queries.reshape(flat), pltpu.HBM),
+        pltpu.with_memory_space_constraint(keys.reshape(flat), pltpu.HBM),
+        pltpu.with_memory_space_constraint(values.reshape(flat), pltpu.HBM),
+        pltpu.with_memory_space_constraint(grad_out.reshape(flat), pltpu.HBM),
+        pltpu.with_memory_space_constraint(gate_weight, pltpu.HBM),
     )
     results = pl.pallas_call(
         finish,

time: 123 us -> 104 us (0.85)
  the two profiles are of different devices: /device:TPU:1 before, /device:TPU:49 now
where the time goes in v1:
time: 104 us
  Pallas kernels  101 us (97%)
  local copies, waits for them, and re-layouts  1.98 us (2%)
    pallas_call x1, Pallas kernels, body(): pl.pallas_call(exchange, out_shape=(jax.ShapeDtypeStruct((4,) + flat, bf1...  98.8 us
    pallas_call x1, Pallas kernels, body(): pl.pallas_call(finish, out_shape=tuple((jax.ShapeDtypeStruct(flat, bf16)...  2.35 us

profile of v1, /device:TPU:49, one launch (start us, length us, event | category | flops | bytes accessed | tf_op | source)
XLA Modules:
  0.0 103.8 jit_solution(17648085458044830457)
XLA Ops:
  0.6 0.0 copy-start
  0.6 0.7 copy-done
  1.3 0.0 copy-start.1
  1.3 0.7 copy-done.1
  2.0 0.0 copy-start.2
  2.0 0.7 copy-done.2
  2.6 98.8 %shard_map.119 = (bf16[4,2,64,1536]{3,2,1,0:T(8,128)(2,1)S(1)}, f32[4,32,384]{2,1,0:T(8,128)S(1)}, f32[32,256]{1,0:T(8,128)S(1)}) custom-call(s32[32]{0:T(128)S(1)} %copy-done.1, s32[32]{0:T(128)S(1)} %copy-done.2, s32[2,16]{1,0:T(2,128)S(1)} %bitcast.17, bf16[2,64,1536]{2,1,0:T(8,128)(2,1)} %bitcast.18, bf16[2,64,1536]{2,1,0:T(8,128)(2,1)} %bitcast.19, ...), custom_call_target="tpu_custom_call" | custom-call | tf_op jit(solution)/shard_map/pallas_call | solution.py:359
  101.4 2.4 %shard_map.120 = (bf16[2,64,1536]{2,1,0:T(8,128)(2,1)}, bf16[2,64,1536]{2,1,0:T(8,128)(2,1)}, bf16[2,64,1536]{2,1,0:T(8,128)(2,1)}, bf16[2,64,1536]{2,1,0:T(8,128)(2,1)}, bf16[256,1536]{1,0:T(8,128)(2,1)}) custom-call(bf16[4,2,64,1536]{3,2,1,0:T(8,128)(2,1)S(1)} %get-tuple-element.13.outs_ref, f32[4,32,384]{2,1,0:T(8,128)S(1)} %get-tuple-element.14.sums_ref, ...), custom_call_target="tpu_custom_call" | custom-call | tf_op jit(solution)/shard_map/pallas_call | solution.py:407
Async XLA Ops:
  0.6 0.7 copy-start
  1.3 0.7 copy-start.1
  2.0 0.7 copy-start.2

commit v2 on v1

--- a/solution.py
+++ b/solution.py
@@ -10,8 +10,6 @@
 
 MESH = pl.DeviceIdType.MESH
 HD = 128
-ZSPLIT = False
-EARLY = False
 ROWS = 16
 CUT = 3
 GROUPS, RANKS = 16, 32
@@ -28,27 +26,42 @@
 
 
 def exchange(
-    frames, steps, order, q_ref, k_ref, v_ref, go_ref, gw_ref,
+    frames_ref, steps_ref, order_ref, q_ref, k_ref, v_ref, go_ref, gw_ref,
     outs_ref, sums_ref, emb_ref,
     raw, stage, moved, rin, ob, xf, of, gwv, gate, part, seen, own, everyone,
-    load_sem, zsend, zrecv, ssem, rsem, osend, orecv, asend, arecv, bsend, brecv,
+    frames, steps, order, load_sem, zsend, zrecv, ssem, rsem, osend, orecv, asend, arecv, bsend, brecv,
 ):
     g = lax.axis_index("grp")
     me = lax.axis_index("seq")
     partner = lax.rem(g + GROUPS // 2, GROUPS)
-    clip = me // 16
-    block = lax.rem(me // 4, 4)
-    heads = lax.rem(me, 4)
+
+    def unit(h, j):
+        ends = (lax.div(h, 2), lax.div(j, 8), lax.rem(j, 8))
+        middle = (lax.div(j, 16), lax.rem(lax.div(j, 4), 4), 8 + lax.rem(j, 4))
+        return tuple(jnp.where(h == 1, m, e) for m, e in zip(middle, ends))
 
     loads = [
         pltpu.make_async_copy(ref, raw.at[t], load_sem.at[t])
         for t, ref in enumerate((q_ref, k_ref, v_ref, go_ref))
     ]
-    mine = pl.ds(pl.multiple_of(heads * SPAN, HD), SPAN)
-    weight = pltpu.make_async_copy(gw_ref.at[:, mine], gwv, load_sem.at[4])
+    weights = [
+        pltpu.make_async_copy(
+            gw_ref.at[:, pl.ds(pl.multiple_of(unit(h, me)[2] * HD, HD), HD)],
+            gwv.at[h],
+            load_sem.at[8 + h],
+        )
+        for h in range(2)
+    ]
+    loads += [
+        pltpu.make_async_copy(ref, small, load_sem.at[5 + t])
+        for t, (ref, small) in enumerate(
+            ((frames_ref, frames), (steps_ref, steps), (order_ref, order))
+        )
+    ]
     for load in loads:
         load.start()
-    weight.start()
+    for weight in weights:
+        weight.start()
 
     barrier = pltpu.get_barrier_semaphore()
 
@@ -82,7 +95,7 @@
             device_id_type=MESH,
         ).start()
 
-    def keep(h, t0, src):
+    def keep(h, j, t0, src):
         pltpu.make_async_copy(src, slot(h, me, t0, src.shape[0]), rsem.at[h]).start()
 
     def migrate(h, src, dst):
@@ -95,73 +108,60 @@
             device_id_type=MESH,
         ).start()
 
-    def arrange(h):
-        for r in range(2):
-            for t in range(4):
-                which = order[r, g] if t < 3 else r
-                for w in range(4):
-                    lanes = slice(w * SPAN + h * HD, w * SPAN + h * HD + HD)
-                    stage[h, r, t, w] = raw[t, which, :, lanes]
+    def arrange(r, tensors, heads):
+        for t in tensors:
+            which = order[r, g] if t < 3 else r
+            for w in heads:
+                stage[r, t, w] = raw[t, which, :, w * HD : (w + 1) * HD]
 
     def plane(h):
-        if not ZSPLIT:
-            migrate(h, stage.at[h, 1, pl.ds(0, 3)], moved.at[h])
-
-        @pl.loop(0, RANKS)
+        def whole(j, to):
+            _, b, w = unit(h, j)
+            to(h, j, 0, stage.at[0, :, w, rows(b)])
+
+        def cotangent(j, to):
+            _, b, w = unit(h, j)
+            to(h, j, 3, stage.at[1, pl.ds(3, 1), w, rows(b)])
+
+        def either(j, to):
+            if h == 0:
+                whole(j, to)
+            elif h == 2:
+                cotangent(j, to)
+            else:
+                pl.when(j < 16)(lambda: whole(j, to))
+                pl.when(j >= 16)(lambda: cotangent(j, to))
+
+        @pl.loop(1, RANKS)
         def _(o):
-            j = lax.rem(me + o, RANKS)
-            b, w = lax.rem(j // 4, 4), lax.rem(j, 4)
-            if ZSPLIT:
-                @pl.when(lax.rem(o, 2) == 0)
-                def _():
-                    pb, pw = o // 8, lax.rem(o // 2, 4)
-                    migrate(
-                        h,
-                        stage.at[h, 1, pl.ds(0, 3), pw, rows(pb)],
-                        moved.at[h, :, pw, rows(pb)],
-                    )
-
-            @pl.when((j < 16) & (o > 0))
-            def _():
-                send(h, j, 0, stage.at[h, 0, pl.ds(0, 4), w, rows(b)])
-
-            @pl.when((j >= 16) & (o > 0))
-            def _():
-                send(h, j, 3, stage.at[h, 1, pl.ds(3, 1), w, rows(b)])
-
-            @pl.when((j < 16) & (o == 0))
-            def _():
-                keep(h, 0, stage.at[h, 0, pl.ds(0, 4), w, rows(b)])
-
-            @pl.when((j >= 16) & (o == 0))
-            def _():
-                keep(h, 3, stage.at[h, 1, pl.ds(3, 1), w, rows(b)])
+            either(lax.rem(me + o, RANKS), send)
+
+        either(me, keep)
 
     def forward(h):
-        pltpu.make_async_copy(moved.at[h], moved.at[h], zrecv.at[h]).wait()
-
-        @pl.loop(0, 16)
+        few = slice(8, 12) if h == 1 else slice(0, 8)
+        came = moved.at[:, few]
+        pltpu.make_async_copy(came, came, zrecv.at[h - 1]).wait()
+
+        def onward(j, to):
+            _, b, w = unit(h, j)
+            to(h, j, 0, moved.at[:, w, rows(b)])
+
+        @pl.loop(0, 16 if h == 1 else RANKS)
         def _(o):
-            i = lax.rem(me + o, 16)
-            j = 16 + i
-            b, w = i // 4, lax.rem(i, 4)
-
-            @pl.when(j != me)
-            def _():
-                send(h, j, 0, moved.at[h, :, w, rows(b)])
-
-            @pl.when(j == me)
-            def _():
-                keep(h, 0, moved.at[h, :, w, rows(b)])
-
-    arrange(0)
+            j = 16 + lax.rem(me + o, 16) if h == 1 else lax.rem(me + o, RANKS)
+            pl.when(j != me)(lambda: onward(j, send))
+            pl.when(j == me)(lambda: onward(j, keep))
+
+    arrange(1, range(3), range(12))
     pl.semaphore_wait(barrier, RANKS - 1 + GROUPS - 1)
+    migrate(0, stage.at[1, pl.ds(0, 3), 8:12], moved.at[:, 8:12])
+    migrate(1, stage.at[1, pl.ds(0, 3), 0:8], moved.at[:, 0:8])
+    arrange(0, range(4), range(8))
     plane(0)
-    arrange(1)
+    arrange(0, range(4), range(8, 12))
+    arrange(1, range(3, 4), range(12))
     plane(1)
-    arrange(2)
-    if EARLY:
-        forward(0)
     plane(2)
 
     half = HD
@@ -175,32 +175,25 @@
     angle = stamp * jnp.exp(-math.log(10000.0) * k / half)
     emb_ref[:, :half] = jnp.cos(angle)
     emb_ref[:, half:] = jnp.sin(angle)
-    weight.wait()
-    gates = lax.dot_general(
-        emb_ref[...],
-        gwv[...].astype(jnp.float32),
-        NN,
-        precision=lax.Precision.HIGHEST,
-        preferred_element_type=jnp.float32,
-    )
-    pick = lax.broadcasted_iota(jnp.int32, gates.shape, 0) == g * 2 + clip
-    gate[...] = jnp.broadcast_to(
-        jnp.sum(jnp.where(pick, gates, 0.0), axis=0, keepdims=True), gate.shape
-    )
-    source = jnp.where(clip == 0, g, partner)
-    count = frames[source * 2 + order[clip, source]]
-
-    if not EARLY:
-        forward(0)
+    for weight in weights:
+        weight.wait()
+    row = lax.broadcasted_iota(jnp.int32, (2 * GROUPS, HD), 0)
+    for h in range(CUT):
+        gates = lax.dot_general(
+            emb_ref[...],
+            gwv[h % 2].astype(jnp.float32),
+            NN,
+            precision=lax.Precision.HIGHEST,
+            preferred_element_type=jnp.float32,
+        )
+        pick = row == g * 2 + unit(h, me)[0]
+        gate[h] = jnp.sum(jnp.where(pick, gates, 0.0), axis=0, keepdims=True)
+
     forward(1)
     forward(2)
 
     line = lax.broadcasted_iota(jnp.int32, (SIDE, SIDE), 0)
     lane = lax.broadcasted_iota(jnp.int32, (SIDE, SIDE), 1)
-    live = (line // RANKS == lane // RANKS) & (lax.rem(lane, RANKS) < count)
-    asks = (
-        lax.rem(lax.broadcasted_iota(jnp.int32, (SIDE, HD), 0), RANKS) < count
-    ).astype(jnp.float32)
     scale = HD ** (-0.5)
 
     @pl.loop(0, CUT)
@@ -213,7 +206,12 @@
             for t in range(4):
                 xf[t, f * ROWS : (f + 1) * ROWS, :] = rin[base + f * 4 + t].astype(jnp.float32)
         lanes = pl.ds(pl.multiple_of(h * HD, HD), HD)
-        gate_h = gate[0:1, lanes]
+        gate_h = gate[h]
+        clip, block, head = unit(h, me)
+        source = jnp.where(clip == 0, g, partner)
+        count = frames[source * 2 + order[clip, source]]
+        live = (line // RANKS == lane // RANKS) & (lax.rem(lane, RANKS) < count)
+        asks = (lax.rem(line, RANKS) < count).astype(jnp.float32)
         total = jnp.zeros((1, HD), jnp.float32)
         for s in range(ROWS // PACK):
 
@@ -271,7 +269,7 @@
             :,
             clip,
             pl.ds(pl.multiple_of(block * ROWS, ROWS), ROWS),
-            pl.ds(pl.multiple_of(heads * SPAN + h * HD, HD), HD),
+            pl.ds(pl.multiple_of(head * HD, HD), HD),
         ]
 
         @pl.loop(1, RANKS)
@@ -291,11 +289,11 @@
     few = seen.at[pl.ds(0, RANKS - 1)]
     pltpu.make_async_copy(few, few, arecv).wait()
     for r in range(2):
-        for w in range(4):
-            acc = seen[r * 16 + w]
-            for b in range(1, 4):
-                acc = acc + seen[r * 16 + b * 4 + w]
-            own[w * 2 + r : w * 2 + r + 1, :] = acc
+        for w in range(12):
+            ranks = [b * 8 + w if w < 8 else r * 16 + b * 4 + w - 8 for b in range(4)]
+            h = 1 if w >= 8 else 2 * r
+            acc = sum(seen[k, :, h * HD : (h + 1) * HD] for k in ranks)
+            own[w // 3 * 2 + r : w // 3 * 2 + r + 1, w % 3 * HD : (w % 3 + 1) * HD] = acc
     everyone[g] = own[...]
 
     @pl.loop(1, GROUPS)
@@ -352,7 +350,6 @@
     clips, fr_dev, spots, width = queries.shape
     flat = (clips, spots, width)
     any_space = pl.BlockSpec(memory_space=pl.ANY)
-    smem = pl.BlockSpec(memory_space=pltpu.SMEM)
     vmem = pl.BlockSpec(memory_space=pltpu.VMEM)
     bf16, f32 = jnp.bfloat16, jnp.float32
     dma = pltpu.SemaphoreType.DMA
@@ -363,25 +360,28 @@
             jax.ShapeDtypeStruct((4, 2 * GROUPS, SPAN), f32),
             jax.ShapeDtypeStruct((2 * GROUPS, 2 * HD), f32),
         ),
-        in_specs=[smem] * 3 + [any_space] * 5,
+        in_specs=[any_space] * 8,
         out_specs=(any_space, vmem, vmem),
         scratch_shapes=[
             pltpu.VMEM((4,) + flat, bf16),
-            pltpu.VMEM((CUT, 2, 4, 4, spots, HD), bf16),
-            pltpu.VMEM((CUT, 3, 4, spots, HD), bf16),
+            pltpu.VMEM((2, 4, 12, spots, HD), bf16),
+            pltpu.VMEM((3, 12, spots, HD), bf16),
             pltpu.VMEM((CUT * RANKS * 4, ROWS, HD), bf16),
             pltpu.VMEM((CUT * RANKS * 4, ROWS, HD), bf16),
             pltpu.VMEM((4, RANKS * ROWS, HD), f32),
             pltpu.VMEM((4, RANKS * ROWS, HD), f32),
-            pltpu.VMEM((gate_weight.shape[0], SPAN), bf16),
-            pltpu.VMEM((8, SPAN), f32),
+            pltpu.VMEM((2, gate_weight.shape[0], HD), bf16),
+            pltpu.VMEM((CUT, 1, HD), f32),
             pltpu.VMEM((1, SPAN), f32),
             pltpu.VMEM((RANKS, 1, SPAN), f32),
             pltpu.VMEM((8, SPAN), f32),
             pltpu.VMEM((GROUPS, 8, SPAN), f32),
-            dma((5,)),
-            dma,
-            dma((CUT,)),
+            pltpu.SMEM((2 * GROUPS,), jnp.int32),
+            pltpu.SMEM((2 * GROUPS,), jnp.int32),
+            pltpu.SMEM((2, GROUPS), jnp.int32),
+            dma((10,)),
+            dma,
+            dma((2,)),
             dma,
             dma((CUT,)),
             dma,
@@ -395,9 +395,9 @@
             collective_id=0, has_side_effects=True, vmem_limit_bytes=32 << 20
         ),
     )(
-        frames,
-        timesteps,
-        order.T,
+        pltpu.with_memory_space_constraint(frames, pltpu.HBM),
+        pltpu.with_memory_space_constraint(timesteps, pltpu.HBM),
+        pltpu.with_memory_space_constraint(order.T, pltpu.HBM),
         pltpu.with_memory_space_constraint(queries.reshape(flat), pltpu.HBM),
         pltpu.with_memory_space_constraint(keys.reshape(flat), pltpu.HBM),
         pltpu.with_memory_space_constraint(values.reshape(flat), pltpu.HBM),

time: 104 us -> 92.1 us (0.89)
  the two profiles are of different devices: /device:TPU:49 before, /device:TPU:1 now
where the time goes in v2:
time: 92.1 us; the launch traced here: 91.1 us
  Pallas kernels  90.5 us (98%)
    pallas_call x1, Pallas kernels, body(): pl.pallas_call(exchange, out_shape=(jax.ShapeDtypeStruct((4,) + flat, bf1...  88.1 us
    pallas_call x1, Pallas kernels, body(): pl.pallas_call(finish, out_shape=tuple((jax.ShapeDtypeStruct(flat, bf16)...  2.35 us

profile of v2, /device:TPU:1, one launch (start us, length us, event | category | flops | bytes accessed | tf_op | source)
XLA Modules:
  0.0 91.1 jit_solution(13746221706394621700)
XLA Ops:
  0.6 88.1 %shard_map.119 = (bf16[4,2,64,1536]{3,2,1,0:T(8,128)(2,1)S(1)}, f32[4,32,384]{2,1,0:T(8,128)S(1)}, f32[32,256]{1,0:T(8,128)S(1)}) custom-call(s32[32]{0:T(128)} %frames_ref.1, s32[32]{0:T(128)} %steps_ref.1, s32[2,16]{1,0:T(2,128)} %bitcast.21, bf16[2,64,1536]{2,1,0:T(8,128)(2,1)} %bitcast.17, bf16[2,64,1536]{2,1,0:T(8,128)(2,1)} %bitcast.18, ...), custom_call_target="tpu_custom_call" | custom-call | tf_op jit(solution)/shard_map/pallas_call | solution.py:356
  88.8 2.4 %shard_map.120 = (bf16[2,64,1536]{2,1,0:T(8,128)(2,1)}, bf16[2,64,1536]{2,1,0:T(8,128)(2,1)}, bf16[2,64,1536]{2,1,0:T(8,128)(2,1)}, bf16[2,64,1536]{2,1,0:T(8,128)(2,1)}, bf16[256,1536]{1,0:T(8,128)(2,1)}) custom-call(bf16[4,2,64,1536]{3,2,1,0:T(8,128)(2,1)S(1)} %get-tuple-element.13.outs_ref, f32[4,32,384]{2,1,0:T(8,128)S(1)} %get-tuple-element.14.sums_ref, ...), custom_call_target="tpu_custom_call" | custom-call | tf_op jit(solution)/shard_map/pallas_call | solution.py:407

commit v3 on v2

--- a/solution.py
+++ b/solution.py
@@ -27,8 +27,8 @@
 
 def exchange(
     frames_ref, steps_ref, order_ref, q_ref, k_ref, v_ref, go_ref, gw_ref,
-    outs_ref, sums_ref, emb_ref,
-    raw, stage, moved, rin, ob, xf, of, gwv, gate, part, seen, own, everyone,
+    outs_ref, gg_ref,
+    emb_ref, raw, stage, moved, rin, ob, xf, of, gwv, gate, part, seen, own, everyone,
     frames, steps, order, load_sem, zsend, zrecv, ssem, rsem, osend, orecv, asend, arecv, bsend, brecv,
 ):
     g = lax.axis_index("grp")
@@ -309,39 +309,38 @@
 
     others = everyone.at[pl.ds(0, GROUPS - 1)]
     pltpu.make_async_copy(others, others, brecv).wait()
-    for i in range(GROUPS):
-        for w in range(4):
-            sums_ref[w, 2 * i : 2 * i + 2, :] = everyone[i, 2 * w : 2 * w + 2, :]
-
-    def drain(sem, ref):
-        pltpu.make_async_copy(ref, ref, sem).wait()
-
-    drain(asend, few)
-    drain(bsend, others)
-
-    drain(zsend, moved)
-    drain(ssem, rin.at[pl.ds(0, CUT * (RANKS - 1) * 4)])
-    drain(osend, rin.at[pl.ds(0, CUT * (RANKS - 1) * 4)])
-    drain(orecv, outs_ref)
-
-
-def finish(outs_ref, sums_ref, emb_ref, o_ref, q_ref, k_ref, v_ref, gg_ref, sem):
-    copies = [
-        pltpu.make_async_copy(outs_ref.at[t], ref, sem.at[t])
-        for t, ref in enumerate((o_ref, q_ref, k_ref, v_ref))
-    ]
-    for copy in copies:
-        copy.start()
-    emb = emb_ref[...]
     for w in range(4):
-        clips = sums_ref[w]
+        clips = jnp.concatenate(
+            [everyone[i, 2 * w : 2 * w + 2, :] for i in range(GROUPS)], axis=0
+        )
         gg_ref[:, w * SPAN : (w + 1) * SPAN] = lax.dot_general(
-            emb,
+            emb_ref[...],
             clips,
             TN,
             precision=lax.Precision.HIGHEST,
             preferred_element_type=jnp.float32,
         ).astype(jnp.bfloat16)
+
+    def drain(sem, ref):
+        pltpu.make_async_copy(ref, ref, sem).wait()
+
+    drain(asend, few)
+    drain(bsend, others)
+
+    drain(zsend, moved)
+    drain(ssem, rin.at[pl.ds(0, CUT * (RANKS - 1) * 4)])
+    drain(osend, rin.at[pl.ds(0, CUT * (RANKS - 1) * 4)])
+    drain(orecv, outs_ref)
+
+
+def finish(outs_ref, gg_in, o_ref, q_ref, k_ref, v_ref, gg_ref, sem):
+    copies = [
+        pltpu.make_async_copy(outs_ref.at[t], ref, sem.at[t])
+        for t, ref in enumerate((o_ref, q_ref, k_ref, v_ref))
+    ]
+    copies.append(pltpu.make_async_copy(gg_in, gg_ref, sem.at[4]))
+    for copy in copies:
+        copy.start()
     for copy in copies:
         copy.wait()
 
@@ -353,16 +352,16 @@
     vmem = pl.BlockSpec(memory_space=pltpu.VMEM)
     bf16, f32 = jnp.bfloat16, jnp.float32
     dma = pltpu.SemaphoreType.DMA
-    outs, sums, emb = pl.pallas_call(
+    outs, product = pl.pallas_call(
         exchange,
         out_shape=(
             jax.ShapeDtypeStruct((4,) + flat, bf16),
-            jax.ShapeDtypeStruct((4, 2 * GROUPS, SPAN), f32),
-            jax.ShapeDtypeStruct((2 * GROUPS, 2 * HD), f32),
+            jax.ShapeDtypeStruct(gate_weight.shape, bf16),
         ),
         in_specs=[any_space] * 8,
-        out_specs=(any_space, vmem, vmem),
+        out_specs=(any_space, vmem),
         scratch_shapes=[
+            pltpu.VMEM((2 * GROUPS, 2 * HD), f32),
             pltpu.VMEM((4,) + flat, bf16),
             pltpu.VMEM((2, 4, 12, spots, HD), bf16),
             pltpu.VMEM((3, 12, spots, HD), bf16),
@@ -408,11 +407,11 @@
         finish,
         out_shape=tuple(jax.ShapeDtypeStruct(flat, bf16) for _ in range(4))
         + (jax.ShapeDtypeStruct(gate_weight.shape, bf16),),
-        in_specs=[any_space, vmem, vmem],
-        out_specs=(any_space,) * 4 + (vmem,),
-        scratch_shapes=[dma((4,))],
+        in_specs=[any_space] * 2,
+        out_specs=(any_space,) * 5,
+        scratch_shapes=[dma((5,))],
         compiler_params=pltpu.CompilerParams(vmem_limit_bytes=32 << 20),
-    )(outs, sums, emb)
+    )(outs, product)
     back = tuple(x.reshape(clips, fr_dev, spots, width) for x in results[:4])
     return back + (results[4],)
 

time: 92.1 us -> 91.7 us (level)
    pallas_call x1, Pallas kernels: 88.1 us -> 89.5 us  [body(): pl.pallas_call(exchange, out_shape=(jax.ShapeDtypeStruct((4,) + flat, bf1...]
where the time goes in v3:
time: 91.7 us; the launch traced here: 91.5 us
  Pallas kernels  90.9 us (99%)
    pallas_call x1, Pallas kernels, body(): pl.pallas_call(exchange, out_shape=(jax.ShapeDtypeStruct((4,) + flat, bf1...  89.5 us

profile of v3, /device:TPU:1, one launch (start us, length us, event | category | flops | bytes accessed | tf_op | source)
XLA Modules:
  0.0 91.5 jit_solution(15439576974849444529)
XLA Ops:
  0.6 89.5 %shard_map.119 = (bf16[4,2,64,1536]{3,2,1,0:T(8,128)(2,1)S(1)}, bf16[256,1536]{1,0:T(8,128)(2,1)S(1)}) custom-call(s32[32]{0:T(128)} %frames_ref.1, s32[32]{0:T(128)} %steps_ref.1, s32[2,16]{1,0:T(2,128)} %bitcast.21, bf16[2,64,1536]{2,1,0:T(8,128)(2,1)} %bitcast.17, bf16[2,64,1536]{2,1,0:T(8,128)(2,1)} %bitcast.18, bf16[2,64,1536]{2,1,0:T(8,128)(2,1)} %bitcast.19, ...), custom_call_target="tpu_custom_call" | custom-call | tf_op jit(solution)/shard_map/pallas_call | solution.py:355
  90.1 1.4 %shard_map.120 = (bf16[2,64,1536]{2,1,0:T(8,128)(2,1)}, bf16[2,64,1536]{2,1,0:T(8,128)(2,1)}, bf16[2,64,1536]{2,1,0:T(8,128)(2,1)}, bf16[2,64,1536]{2,1,0:T(8,128)(2,1)}, bf16[256,1536]{1,0:T(8,128)(2,1)}) custom-call(bf16[4,2,64,1536]{3,2,1,0:T(8,128)(2,1)S(1)} %get-tuple-element.12.outs_ref, bf16[256,1536]{1,0:T(8,128)(2,1)S(1)} %get-tuple-element.13.gg_in), custom_call_target="tpu_custom_call" | custom-call | tf_op jit(solution)/shard_map/pallas_call | solution.py:406

commit v4 on v3

--- a/solution.py
+++ b/solution.py
@@ -79,6 +79,10 @@
     for load in loads:
         load.wait()
 
+    def peer(o):
+        y, x = lax.div(me, 4) + 3 * lax.rem(o, 8), lax.rem(me, 4) + lax.div(o, 8) + lax.rem(o, 8)
+        return lax.rem(y, 8) * 4 + lax.rem(x, 4)
+
     def rows(b):
         return pl.ds(pl.multiple_of(b * ROWS, ROWS), ROWS)
 
@@ -134,7 +138,7 @@
 
         @pl.loop(1, RANKS)
         def _(o):
-            either(lax.rem(me + o, RANKS), send)
+            either(peer(o), send)
 
         either(me, keep)
 
@@ -149,7 +153,7 @@
 
         @pl.loop(0, 16 if h == 1 else RANKS)
         def _(o):
-            j = 16 + lax.rem(me + o, 16) if h == 1 else lax.rem(me + o, RANKS)
+            j = 16 + lax.rem(me + o, 16) if h == 1 else peer(o)
             pl.when(j != me)(lambda: onward(j, send))
             pl.when(j == me)(lambda: onward(j, keep))
 
@@ -274,7 +278,7 @@
 
         @pl.loop(1, RANKS)
         def _(o):
-            f = lax.rem(me + o, RANKS)
+            f = peer(o)
             pltpu.make_async_remote_copy(
                 src_ref=ob.at[pl.ds(base + f * 4, 4)],
                 dst_ref=place,

time: 91.7 us -> 91.8 us (level)
  no operation moved by 1% of the time
where the time goes in v4:
time: 91.8 us; the launch traced here: 91.6 us
  Pallas kernels  91 us (99%)
    pallas_call x1, Pallas kernels, body(): pl.pallas_call(exchange, out_shape=(jax.ShapeDtypeStruct((4,) + flat, bf1...  89.5 us

profile of v4, /device:TPU:1, one launch (start us, length us, event | category | flops | bytes accessed | tf_op | source)
XLA Modules:
  0.0 91.6 jit_solution(5267867969667049067)
XLA Ops:
  0.6 89.5 %shard_map.119 = (bf16[4,2,64,1536]{3,2,1,0:T(8,128)(2,1)S(1)}, bf16[256,1536]{1,0:T(8,128)(2,1)S(1)}) custom-call(s32[32]{0:T(128)} %frames_ref.1, s32[32]{0:T(128)} %steps_ref.1, s32[2,16]{1,0:T(2,128)} %bitcast.21, bf16[2,64,1536]{2,1,0:T(8,128)(2,1)} %bitcast.17, bf16[2,64,1536]{2,1,0:T(8,128)(2,1)} %bitcast.18, bf16[2,64,1536]{2,1,0:T(8,128)(2,1)} %bitcast.19, ...), custom_call_target="tpu_custom_call" | custom-call | tf_op jit(solution)/shard_map/pallas_call | solution.py:359
  90.2 1.4 %shard_map.120 = (bf16[2,64,1536]{2,1,0:T(8,128)(2,1)}, bf16[2,64,1536]{2,1,0:T(8,128)(2,1)}, bf16[2,64,1536]{2,1,0:T(8,128)(2,1)}, bf16[2,64,1536]{2,1,0:T(8,128)(2,1)}, bf16[256,1536]{1,0:T(8,128)(2,1)}) custom-call(bf16[4,2,64,1536]{3,2,1,0:T(8,128)(2,1)S(1)} %get-tuple-element.12.outs_ref, bf16[256,1536]{1,0:T(8,128)(2,1)S(1)} %get-tuple-element.13.gg_in), custom_call_target="tpu_custom_call" | custom-call | tf_op jit(solution)/shard_map/pallas_call | solution.py:410
